TPU v7x, 32 devices: a whole 2x2x4 slice. The times are simulated.
32 devices in a mesh: gx: 4 (over y, x), gy: 8 (over z, core).
Axes of the slice: x: 2, y: 2, z: 4, core: 2. Of those that a mesh axis runs over, the one named last changes fastest.
Arguments:
- right_side: float32 [70, 96, 1024], P(None, 'gx', 'gy'), may hold values from -6 to 6
- helm_coef: float32 [70, 96, 1024], P(None, 'gx', 'gy'), may hold values from 0.5 to 4
- vert_coef: float32 [71], replicated, may hold values from 1 to 10
- block_inverse: float32 [4, 5, 14, 14], replicated, may hold values from -0.1 to 0.45, as said below
- edge_flip: int32 [4, 8, 4], P('gx', 'gy'), may hold values 0 or 1
Outputs:
- correction: float32 [70, 96, 1024], P(None, 'gx', 'gy')
Inputs may be any that keep to these rules, and one draw needn't show every extreme that they name: `block_inverse`: each block's diagonal entries are positive and larger than the off-diagonal ones.
All inputs are finite; a program needn't handle non-finite values. No bound on the sum of `edge_flip` on one device may be relied on, other than what follows from the above.
Results may differ from a plain program's by a relative error of at most 0.0001.
Values sent between devices are 32-bit elements; how exact they have to be, the bound alone decides.
A program may use at most 128 MiB of HBM per device.

v0:
```python
import functools
import jax
import jax.numpy as jnp
from jax import lax
from jax.experimental import pallas as pl
from jax.experimental.pallas import tpu as pltpu
from jax.sharding import PartitionSpec as P

BLK = 14
LEVELS = 4
LANES = 128
MESH = pl.DeviceIdType.MESH
BF = jnp.bfloat16
F32 = jnp.float32


def split2(x):
    hi = x.astype(BF).astype(F32)
    return hi, x - hi


def permute(x, matrix):
    depth = x.shape[0]
    hi, lo = split2(x)
    both = jnp.concatenate([hi, lo], axis=0).astype(BF)
    out = jnp.dot(both, matrix, preferred_element_type=F32)
    return out[:depth] + out[depth:]


def block_dot(binv, r):
    hi, lo = split2(r)
    cat = jnp.concatenate([hi, lo, hi, jnp.zeros((8, r.shape[1]), F32)], axis=0).astype(BF)
    return jnp.dot(binv, cat, preferred_element_type=F32)


def kernel(n_gx, n_gy, rows0, depth, flip_ref, s_in, c_in, kz_ref, binv_ref, out_ref,
           va0, va1, va2, va3, vb0, vb1, vb2, vb3, s0, s1, s2, s3, d0, d1, d2, d3,
           edge, held, px, py, resm, prom, send_sem, recv_sem):
    va, vb = (va0, va1, va2, va3), (vb0, vb1, vb2, vb3)
    src, dia = (s0, s1, s2, s3), (d0, d1, d2, d3)
    gx, gy = lax.axis_index("gx"), lax.axis_index("gy")
    peers = (
        (lax.rem(gx + n_gx - 1, n_gx), gy),
        (lax.rem(gx + 1, n_gx), gy),
        (gx, lax.rem(gy + n_gy - 1, n_gy)),
        (gx, lax.rem(gy + 1, n_gy)),
    )
    barrier = pltpu.get_barrier_semaphore()
    for peer in peers:
        pl.semaphore_signal(barrier, inc=1, device_id=peer, device_id_type=MESH)

    nrow = [rows0 >> l for l in range(LEVELS)]
    ncol = [LANES >> l for l in range(LEVELS)]
    lane = lax.broadcasted_iota(jnp.int32, (depth, LANES), 1)
    ki = lax.broadcasted_iota(jnp.int32, (LANES, LANES), 0)
    mi = lax.broadcasted_iota(jnp.int32, (LANES, LANES), 1)
    flips = [flip_ref[0, 0, s] > 0 for s in range(4)]

    def as_matrix(hit, value=1.0):
        return jnp.where(hit, value, 0.0).astype(F32).astype(BF)

    for l in range(LEVELS):
        r, c = nrow[l], ncol[l]
        for side in range(2):
            spot = jnp.where(flips[side], c - 1 - mi, mi)
            px[l, side] = as_matrix((ki == spot) & (mi < c))
        xm = mi >> 1
        from_low = (2 * jnp.where(flips[2], r - 1 - xm, xm) + c) & (LANES - 1)
        py[l, 0:LANES, :] = as_matrix((ki == from_low) & ((mi & 1) == 1) & (xm < r))
        xh = ((mi - c) & (LANES - 1)) >> 1
        from_high = 2 * jnp.where(flips[3], r - 1 - xh, xh) + 1
        py[l, LANES:, :] = as_matrix((ki == from_high) & ((mi & 1) == 0) & (xh < r))
    for l in range(LEVELS - 1):
        resm[l] = as_matrix(((ki >> 1) == mi) & (mi < ncol[l + 1]), 0.25)
        prom[l] = as_matrix(((mi >> 1) == ki) & (mi < ncol[l]))

    for l in range(LEVELS):
        for buf in (va[l], vb[l]):
            buf[0] = jnp.zeros((depth, LANES), F32)
            buf[nrow[l] + 1] = jnp.zeros((depth, LANES), F32)

    group = [4, 4, 6, 3]

    def each_group(l, body, carry=0):
        g = group[l] if nrow[l] % group[l] == 0 else 1
        trips = nrow[l] // g
        if trips == 1:
            return body(0, g, carry)
        return lax.fori_loop(0, trips, lambda i, acc: body(i * g, g, acc), carry)

    def extract(acc, row, x, c):
        turned = pltpu.roll(row, 2 * x + 1, 1)
        hit = (lane == 2 * x + 1) | (lane == ((2 * x + c) & (LANES - 1)))
        return jnp.where(hit, turned, acc)

    def ends(c):
        return (lane == 0) | (lane == c - 1)

    def insert(tile, x, c):
        return jnp.where(ends(c), pltpu.roll(tile, (LANES - 1) - 2 * x, 1), 0.0)

    def send(k, l, v):
        r = nrow[l]
        plan = ((v.at[1], 0, 1), (v.at[r], 1, 0), (edge, 2, 3), (edge, 3, 2))
        copies = []
        for ref, to, slot in plan:
            copies.append(pltpu.make_async_remote_copy(
                src_ref=ref, dst_ref=held.at[k, slot], send_sem=send_sem.at[k, slot],
                recv_sem=recv_sem.at[k, slot], device_id=peers[to], device_id_type=MESH))
            copies[-1].start()
        return copies

    up, down = kz_ref[0], kz_ref[1]

    def partial(l, v, x):
        c = ncol[l]
        mid = v[x + 1]
        r = src[l][x] - dia[l][x] * mid + (v[x] + v[x + 2])
        r = r + jnp.where(lane == 0, 0.0, pltpu.roll(mid, 1, 1))
        r = r + jnp.where(lane == c - 1, 0.0, pltpu.roll(mid, LANES - 1, 1))
        r = r + up * pltpu.roll(mid, depth - 1, 0) + down * pltpu.roll(mid, 1, 0)
        return r, mid

    def halos(k, l):
        low = permute(held[k, 0], px[l, 0])
        high = permute(held[k, 1], px[l, 1])
        beside = permute(jnp.concatenate([held[k, 2], held[k, 3]], axis=1), py[l])
        return low, high, beside

    count = [0]

    def from_zero(l, v):
        def body(x0, g, acc):
            rr = jnp.concatenate([src[l][x0 + j] for j in range(g)], axis=1)
            d = block_dot(binv_ref[l], rr)
            for j in range(g):
                row = d[:, j * LANES:(j + 1) * LANES]
                v[x0 + j + 1] = row
                acc = extract(acc, row, x0 + j, ncol[l])
            return acc
        edge[...] = each_group(l, body, jnp.zeros((depth, LANES), F32))

    def relax(l, v, w, pending=None):
        k = count[0]
        count[0] += 1
        copies = send(k, l, v)
        settle(l, v, pending)

        def body(x0, g, acc):
            parts = [partial(l, v, x0 + j) for j in range(g)]
            d = block_dot(binv_ref[l], jnp.concatenate([p[0] for p in parts], axis=1))
            for j in range(g):
                row = parts[j][1] + d[:, j * LANES:(j + 1) * LANES]
                w[x0 + j + 1] = row
                acc = extract(acc, row, x0 + j, ncol[l])
            return acc

        acc = each_group(l, body, jnp.zeros((depth, LANES), F32))
        for copy in copies:
            copy.wait()
        r, c = nrow[l], ncol[l]
        corr = block_dot(binv_ref[l], jnp.concatenate(halos(k, l), axis=1))
        low, high, beside = (corr[:, j * LANES:(j + 1) * LANES] for j in range(3))
        w[1] = w[1] + low + insert(beside, 0, c)
        w[r] = w[r] + high + insert(beside, r - 1, c)
        acc = acc + beside
        zero = jnp.zeros_like(acc)
        acc = acc + extract(zero, low, 0, c) + extract(zero, high, r - 1, c)
        edge[...] = acc
        return beside

    def settle(l, v, beside):
        if beside is None:
            return
        c = ncol[l]
        for x in range(1, nrow[l] - 1):
            v[x + 1] = v[x + 1] + insert(beside, x, c)

    def residual(l, v, w, pending):
        k = count[0]
        count[0] += 1
        copies = send(k, l, v)
        settle(l, v, pending)

        def body(x0, g, acc):
            for j in range(g):
                w[x0 + j + 1] = partial(l, v, x0 + j)[0]
            return acc

        each_group(l, body)
        for copy in copies:
            copy.wait()
        r, c = nrow[l], ncol[l]
        low, high, beside = halos(k, l)
        w[1] = w[1] + low
        w[r] = w[r] + high
        for x in range(0, r, 2):
            pair = w[x + 1] + w[x + 2] + insert(beside, x, c) + insert(beside, x + 1, c)
            src[l + 1][x // 2] = permute(pair, resm[l])

    def add_coarse(l, v, coarse):
        acc = jnp.zeros((depth, LANES), F32)
        for x in range(nrow[l + 1]):
            fine = permute(coarse[x + 1], prom[l])
            for j in (2 * x, 2 * x + 1):
                row = v[j + 1] + fine
                v[j + 1] = row
                acc = extract(acc, row, j, ncol[l])
        edge[...] = acc

    def cycle(l):
        a, b = va[l], vb[l]
        from_zero(l, a)
        if l == LEVELS - 1:
            p = relax(l, a, b)
            p = relax(l, b, a, p)
            p = relax(l, a, b, p)
            settle(l, b, p)
            return b
        p = relax(l, a, b)
        residual(l, b, a, p)
        add_coarse(l, b, cycle(l + 1))
        p = relax(l, b, a)
        p = relax(l, a, b, p)
        settle(l, b, p)
        return b

    for x in range(rows0):
        src[0][x] = s_in[x] * 16.0
        dia[0][x] = c_in[x] + kz_ref[2]
    for l in range(LEVELS - 1):
        for x in range(nrow[l + 1]):
            dia[l + 1][x] = permute(dia[l][2 * x] + dia[l][2 * x + 1], resm[l])
    pl.semaphore_wait(barrier, 4)
    v = cycle(0)
    for x in range(rows0):
        out_ref[x] = v[x + 1]


def on_device(n_gx, n_gy, right_side, helm_coef, vert_coef, block_inverse, edge_flip):
    nz, rows, cols = right_side.shape
    depth = -(-nz // 8) * 8
    pad = depth - nz
    lay = lambda a: jnp.pad(a.transpose(1, 0, 2), ((0, 0), (0, pad), (0, 0)))
    s, c = lay(right_side), lay(helm_coef)
    kz = jnp.stack([vert_coef[1:], vert_coef[:-1], 4.0 + vert_coef[1:] + vert_coef[:-1]])
    kz = jnp.broadcast_to(jnp.pad(kz, ((0, 0), (0, pad)))[:, :, None], (3, depth, LANES))
    nblk = nz // BLK
    eye = jnp.eye(nblk, dtype=F32)[None, :, None, :, None]
    full = (block_inverse[:, :, :, None, :] * eye).reshape(LEVELS, nz, nz) * 0.0625
    full = jnp.pad(full, ((0, 0), (0, pad), (0, pad)))
    hi = lax.reduce_precision(full, 8, 7)
    binv = jnp.concatenate([hi, hi, full - hi, jnp.zeros((LEVELS, depth, 8), F32)], axis=2).astype(BF)

    tile = lambda r: pltpu.VMEM((r, depth, LANES), F32)
    rl = [rows >> l for l in range(LEVELS)]
    steps = 4 * (LEVELS - 1) + 3
    vm = pl.BlockSpec(memory_space=pltpu.VMEM)
    out = pl.pallas_call(
        functools.partial(kernel, n_gx, n_gy, rows, depth),
        out_shape=jax.ShapeDtypeStruct((rows, depth, LANES), F32),
        in_specs=[pl.BlockSpec(memory_space=pltpu.SMEM), vm, vm, vm, vm],
        out_specs=vm,
        scratch_shapes=[tile(r + 2) for r in rl] * 2 + [tile(r) for r in rl] * 2 + [
            pltpu.VMEM((depth, LANES), F32),
            pltpu.VMEM((steps, 4, depth, LANES), F32),
            pltpu.VMEM((LEVELS, 2, LANES, LANES), BF),
            pltpu.VMEM((LEVELS, 2 * LANES, LANES), BF),
            pltpu.VMEM((LEVELS - 1, LANES, LANES), BF),
            pltpu.VMEM((LEVELS - 1, LANES, LANES), BF),
            pltpu.SemaphoreType.DMA((steps, 4)),
            pltpu.SemaphoreType.DMA((steps, 4)),
        ],
        compiler_params=pltpu.CompilerParams(
            collective_id=0, has_side_effects=True, vmem_limit_bytes=40 * 1024 * 1024),
    )(edge_flip, s, c, kz, binv)
    return out[:, :nz, :].transpose(1, 0, 2)


def solution(mesh):
    placed = (P(None, "gx", "gy"), P(None, "gx", "gy"), P(), P(), P("gx", "gy", None))
    return jax.shard_map(
        functools.partial(on_device, mesh.shape["gx"], mesh.shape["gy"]),
        mesh=mesh, in_specs=placed, out_specs=P(None, "gx", "gy"), check_vma=False)
```

profile of v0, /device:TPU:0, one launch (start us, length us, event | category | flops | bytes accessed | tf_op | source)
XLA Modules:
  0.0 79.4 jit_solution(4747360023382418263)
XLA Ops:
  0.0 0.8 %slice_bitcast_fusion.2 = (f32[1,70]{1,0:T(1,128)S(1)}, f32[1,70]{1,0:T(1,128)S(1)}, f32[1,70]{1,0:T(1,128)S(1)}) fusion(f32[71]{0:T(128)} %param.7), kind=kLoop, calls=%fused_computation.15 | loop fusion | flops 140 | bytes 1400 | tf_op jit(solution)/shard_map/stack | solution.py:246
  0.8 0.1 broadcast_in_dim.4.kz_ref
  0.9 0.9 %copy.12 = f32[4,5,14,14]{3,2,1,0:T(8,128)S(1)} copy(f32[4,5,14,14]{3,0,2,1:T(4,128)} %param.8) | data formatting | bytes 31360 | tf_op args[3]
  1.8 0.1 mul.26
  1.9 0.0 copy-start.1
  1.9 0.2 mul.27
  2.2 0.1 mul.28
  2.3 0.1 mul.29
  2.5 0.1 pad.22.clone
  2.6 0.1 maximum_maximum_fusion.binv_ref
  2.7 0.4 copy-done.1
  3.1 0.2 copy.17
  3.3 0.0 copy-start.2
  3.3 0.1 pad.15.s_in
  3.3 1.1 %copy-done.2 = f32[70,24,128]{2,1,0:T(8,128)S(1)} copy-done((f32[70,24,128]{2,1,0:T(8,128)S(1)}, f32[70,24,128]{2,1,0:T(8,128)}, u32[]{:S(2)}) %copy-start.2) | copy-done | bytes 860184
  4.4 0.2 copy.16
  4.6 0.0 copy-start
  4.6 0.1 pad.16.c_in
  4.7 0.6 copy-done
  5.3 73.0 %shard_map.55 = f32[24,72,128]{2,1,0:T(8,128)S(1)} custom-call(s32[1,1,4]{2,1,0:T(1,128)S(1)} %copy-done, f32[24,72,128]{2,1,0:T(8,128)S(1)} %pad.15.s_in, f32[24,72,128]{2,1,0:T(8,128)S(1)} %pad.16.c_in, f32[3,72,128]{2,1,0:T(8,128)S(1)} %broadcast_in_dim.4.kz_ref, bf16[4,72,224]{2,1,0:T(8,128)(2,1)S(1)} %maximum_maximum_fusion.binv_ref), custom_call_target="tpu_custom_call" | custom-call | tf_op jit(solution)/shard_map/pallas_call | solution.py:259
  78.3 0.1 slice_bitcast_fusion
  78.3 1.1 %copy.13 = f32[70,24,128]{2,1,0:T(8,128)} copy(f32[70,24,128]{2,0,1:T(8,128)S(1)} %slice_bitcast_fusion) | data formatting | bytes 1720320 | tf_op jit(solution)/shard_map/transpose | solution.py:277
  (5 shorter events, 0.1 us)
Async XLA Ops:
  1.9 1.2 %copy-start.1 = (f32[70,24,128]{2,1,0:T(8,128)S(1)}, f32[70,24,128]{2,1,0:T(8,128)}, u32[]{:S(2)}) copy-start(f32[70,24,128]{2,1,0:T(8,128)} %param.5) | copy-start | bytes 2580484
  3.3 1.2 %copy-start.2 = (f32[70,24,128]{2,1,0:T(8,128)S(1)}, f32[70,24,128]{2,1,0:T(8,128)}, u32[]{:S(2)}) copy-start(f32[70,24,128]{2,1,0:T(8,128)} %param.6) | copy-start | bytes 2580484
  4.6 0.7 copy-start
where the time goes:
time: 79.6 us; the launch traced here: 79.4 us
  Pallas kernels  73 us (92%)
  local copies, waits for them, and re-layouts  5.27 us (7%)
  other arithmetic  1 us (1%)
    pallas_call x1, Pallas kernels, on_device(): pl.pallas_call(functools.partial(kernel, n_gx, n_gy, rows, depth), out_sh...  73 us
    unnamed x9, local copies, waits for them, and re-layouts  3.35 us

commit v1 on v0

--- a/solution.py
+++ b/solution.py
@@ -27,6 +27,32 @@
     return out[:depth] + out[depth:]
 
 
+FOLD_ROW = (1, 2, 4, 4)
+FOLD_END = (2, 4, 4, 4)
+
+
+def pack(tile, fold):
+    width = LANES // fold
+    units = tile.shape[0] // 8
+    outs = []
+    for first in range(0, units, fold):
+        acc = tile[8 * first:8 * first + 8]
+        for q in range(1, min(fold, units - first)):
+            part = tile[8 * (first + q):8 * (first + q) + 8]
+            acc = acc + pltpu.roll(part, width * q, 1)
+        outs.append(acc)
+    return jnp.concatenate(outs, axis=0)
+
+
+def unpack(packed, matrix, depth, fold):
+    wide = permute(packed, matrix)
+    parts = []
+    for unit in range(depth // 8):
+        j, q = divmod(unit, fold)
+        parts.append(wide[8 * j:8 * j + 8, LANES * q:LANES * (q + 1)])
+    return jnp.concatenate(parts, axis=0)
+
+
 def block_dot(binv, r):
     hi, lo = split2(r)
     cat = jnp.concatenate([hi, lo, hi, jnp.zeros((8, r.shape[1]), F32)], axis=0).astype(BF)
@@ -34,6 +60,7 @@
 
 
 def kernel(n_gx, n_gy, rows0, depth, flip_ref, s_in, c_in, kz_ref, binv_ref, out_ref,
+           stage_s, stage_c, row_send, io_sem,
            va0, va1, va2, va3, vb0, vb1, vb2, vb3, s0, s1, s2, s3, d0, d1, d2, d3,
            edge, held, px, py, resm, prom, send_sem, recv_sem):
     va, vb = (va0, va1, va2, va3), (vb0, vb1, vb2, vb3)
@@ -45,6 +72,12 @@
         (gx, lax.rem(gy + n_gy - 1, n_gy)),
         (gx, lax.rem(gy + 1, n_gy)),
     )
+    loads = []
+    for x in range(rows0):
+        loads.append(pltpu.make_async_copy(s_in.at[:, x, 0, :], stage_s.at[x], io_sem.at[0, x]))
+        loads.append(pltpu.make_async_copy(c_in.at[:, x, 0, :], stage_c.at[x], io_sem.at[1, x]))
+    for load in loads:
+        load.start()
     barrier = pltpu.get_barrier_semaphore()
     for peer in peers:
         pl.semaphore_signal(barrier, inc=1, device_id=peer, device_id_type=MESH)
@@ -63,13 +96,18 @@
         r, c = nrow[l], ncol[l]
         for side in range(2):
             spot = jnp.where(flips[side], c - 1 - mi, mi)
-            px[l, side] = as_matrix((ki == spot) & (mi < c))
+            for q in range(FOLD_ROW[l]):
+                px[l, side, :, LANES * q:LANES * (q + 1)] = as_matrix(
+                    (ki == spot + q * (LANES // FOLD_ROW[l])) & (mi < c))
         xm = mi >> 1
-        from_low = (2 * jnp.where(flips[2], r - 1 - xm, xm) + c) & (LANES - 1)
-        py[l, 0:LANES, :] = as_matrix((ki == from_low) & ((mi & 1) == 1) & (xm < r))
         xh = ((mi - c) & (LANES - 1)) >> 1
-        from_high = 2 * jnp.where(flips[3], r - 1 - xh, xh) + 1
-        py[l, LANES:, :] = as_matrix((ki == from_high) & ((mi & 1) == 0) & (xh < r))
+        for q in range(FOLD_END[l]):
+            at = q * (LANES // FOLD_END[l])
+            cols = slice(LANES * q, LANES * (q + 1))
+            from_low = (2 * jnp.where(flips[2], r - 1 - xm, xm) + c + at) & (LANES - 1)
+            py[l, 0:LANES, cols] = as_matrix((ki == from_low) & ((mi & 1) == 1) & (xm < r))
+            from_high = (2 * jnp.where(flips[3], r - 1 - xh, xh) + 1 + at) & (LANES - 1)
+            py[l, LANES:, cols] = as_matrix((ki == from_high) & ((mi & 1) == 0) & (xh < r))
     for l in range(LEVELS - 1):
         resm[l] = as_matrix(((ki >> 1) == mi) & (mi < ncol[l + 1]), 0.25)
         prom[l] = as_matrix(((mi >> 1) == ki) & (mi < ncol[l]))
@@ -99,13 +137,31 @@
     def insert(tile, x, c):
         return jnp.where(ends(c), pltpu.roll(tile, (LANES - 1) - 2 * x, 1), 0.0)
 
+    def row_size(l):
+        return 8 * -(-(depth // 8) // FOLD_ROW[l])
+
+    def end_size(l):
+        return 8 * -(-(depth // 8) // FOLD_END[l])
+
+    def put_ends(l, tile):
+        edge[0:end_size(l)] = pack(tile, FOLD_END[l])
+
     def send(k, l, v):
         r = nrow[l]
-        plan = ((v.at[1], 0, 1), (v.at[r], 1, 0), (edge, 2, 3), (edge, 3, 2))
+        if l == 0:
+            rows = (v.at[1], v.at[r])
+        else:
+            size = row_size(l)
+            for side, at in ((0, 1), (1, r)):
+                row_send[side, 0:size] = pack(jnp.where(lane < ncol[l], v[at], 0.0), FOLD_ROW[l])
+            rows = (row_send.at[0, pl.ds(0, size)], row_send.at[1, pl.ds(0, size)])
+        size = end_size(l)
+        ends_ref = edge.at[pl.ds(0, size)]
         copies = []
-        for ref, to, slot in plan:
+        for ref, to, slot in ((rows[0], 0, 1), (rows[1], 1, 0), (ends_ref, 2, 3), (ends_ref, 3, 2)):
+            count_z = row_size(l) if to < 2 else size
             copies.append(pltpu.make_async_remote_copy(
-                src_ref=ref, dst_ref=held.at[k, slot], send_sem=send_sem.at[k, slot],
+                src_ref=ref, dst_ref=held.at[k, slot, pl.ds(0, count_z)], send_sem=send_sem.at[k, slot],
                 recv_sem=recv_sem.at[k, slot], device_id=peers[to], device_id_type=MESH))
             copies[-1].start()
         return copies
@@ -122,9 +178,13 @@
         return r, mid
 
     def halos(k, l):
-        low = permute(held[k, 0], px[l, 0])
-        high = permute(held[k, 1], px[l, 1])
-        beside = permute(jnp.concatenate([held[k, 2], held[k, 3]], axis=1), py[l])
+        size = row_size(l)
+        low, high = (
+            unpack(held[k, side, 0:size], px[l, side, :, 0:LANES * FOLD_ROW[l]], depth, FOLD_ROW[l])
+            for side in range(2))
+        size = end_size(l)
+        both = jnp.concatenate([held[k, 2, 0:size], held[k, 3, 0:size]], axis=1)
+        beside = unpack(both, py[l, :, 0:LANES * FOLD_END[l]], depth, FOLD_END[l])
         return low, high, beside
 
     count = [0]
@@ -138,7 +198,7 @@
                 v[x0 + j + 1] = row
                 acc = extract(acc, row, x0 + j, ncol[l])
             return acc
-        edge[...] = each_group(l, body, jnp.zeros((depth, LANES), F32))
+        put_ends(l, each_group(l, body, jnp.zeros((depth, LANES), F32)))
 
     def relax(l, v, w, pending=None):
         k = count[0]
@@ -166,7 +226,7 @@
         acc = acc + beside
         zero = jnp.zeros_like(acc)
         acc = acc + extract(zero, low, 0, c) + extract(zero, high, r - 1, c)
-        edge[...] = acc
+        put_ends(l, acc)
         return beside
 
     def settle(l, v, beside):
@@ -206,7 +266,7 @@
                 row = v[j + 1] + fine
                 v[j + 1] = row
                 acc = extract(acc, row, j, ncol[l])
-        edge[...] = acc
+        put_ends(l, acc)
 
     def cycle(l):
         a, b = va[l], vb[l]
@@ -225,24 +285,32 @@
         settle(l, b, p)
         return b
 
+    for load in loads:
+        load.wait()
+    nz = stage_s.shape[1]
+    tail = jnp.zeros((depth - nz, LANES), F32)
     for x in range(rows0):
-        src[0][x] = s_in[x] * 16.0
-        dia[0][x] = c_in[x] + kz_ref[2]
+        src[0][x] = jnp.concatenate([stage_s[x] * 16.0, tail], axis=0)
+        dia[0][x] = jnp.concatenate([stage_c[x], tail], axis=0) + kz_ref[2]
     for l in range(LEVELS - 1):
         for x in range(nrow[l + 1]):
             dia[l + 1][x] = permute(dia[l][2 * x] + dia[l][2 * x + 1], resm[l])
     pl.semaphore_wait(barrier, 4)
     v = cycle(0)
+    stores = []
     for x in range(rows0):
-        out_ref[x] = v[x + 1]
+        stage_s[x] = v[x + 1][0:nz]
+        stores.append(pltpu.make_async_copy(stage_s.at[x], out_ref.at[:, x, 0, :], io_sem.at[0, x]))
+        stores[-1].start()
+    for store in stores:
+        store.wait()
 
 
 def on_device(n_gx, n_gy, right_side, helm_coef, vert_coef, block_inverse, edge_flip):
     nz, rows, cols = right_side.shape
     depth = -(-nz // 8) * 8
     pad = depth - nz
-    lay = lambda a: jnp.pad(a.transpose(1, 0, 2), ((0, 0), (0, pad), (0, 0)))
-    s, c = lay(right_side), lay(helm_coef)
+    s, c = (a.reshape(nz, rows, 1, cols) for a in (right_side, helm_coef))
     kz = jnp.stack([vert_coef[1:], vert_coef[:-1], 4.0 + vert_coef[1:] + vert_coef[:-1]])
     kz = jnp.broadcast_to(jnp.pad(kz, ((0, 0), (0, pad)))[:, :, None], (3, depth, LANES))
     nblk = nz // BLK
@@ -255,17 +323,23 @@
     tile = lambda r: pltpu.VMEM((r, depth, LANES), F32)
     rl = [rows >> l for l in range(LEVELS)]
     steps = 4 * (LEVELS - 1) + 3
+    hbm = pl.BlockSpec(memory_space=pl.ANY)
     vm = pl.BlockSpec(memory_space=pltpu.VMEM)
     out = pl.pallas_call(
         functools.partial(kernel, n_gx, n_gy, rows, depth),
-        out_shape=jax.ShapeDtypeStruct((rows, depth, LANES), F32),
-        in_specs=[pl.BlockSpec(memory_space=pltpu.SMEM), vm, vm, vm, vm],
-        out_specs=vm,
-        scratch_shapes=[tile(r + 2) for r in rl] * 2 + [tile(r) for r in rl] * 2 + [
+        out_shape=jax.ShapeDtypeStruct((nz, rows, 1, LANES), F32),
+        in_specs=[pl.BlockSpec(memory_space=pltpu.SMEM), hbm, hbm, vm, vm],
+        out_specs=hbm,
+        scratch_shapes=[
+            pltpu.VMEM((rows, nz, LANES), F32),
+            pltpu.VMEM((rows, nz, LANES), F32),
+            pltpu.VMEM((2, depth, LANES), F32),
+            pltpu.SemaphoreType.DMA((2, rows)),
+        ] + [tile(r + 2) for r in rl] * 2 + [tile(r) for r in rl] * 2 + [
             pltpu.VMEM((depth, LANES), F32),
             pltpu.VMEM((steps, 4, depth, LANES), F32),
-            pltpu.VMEM((LEVELS, 2, LANES, LANES), BF),
-            pltpu.VMEM((LEVELS, 2 * LANES, LANES), BF),
+            pltpu.VMEM((LEVELS, 2, LANES, LANES * max(FOLD_ROW)), BF),
+            pltpu.VMEM((LEVELS, 2 * LANES, LANES * max(FOLD_END)), BF),
             pltpu.VMEM((LEVELS - 1, LANES, LANES), BF),
             pltpu.VMEM((LEVELS - 1, LANES, LANES), BF),
             pltpu.SemaphoreType.DMA((steps, 4)),
@@ -274,7 +348,7 @@
         compiler_params=pltpu.CompilerParams(
             collective_id=0, has_side_effects=True, vmem_limit_bytes=40 * 1024 * 1024),
     )(edge_flip, s, c, kz, binv)
-    return out[:, :nz, :].transpose(1, 0, 2)
+    return out.reshape(nz, rows, cols)
 
 
 def solution(mesh):

time: 79.6 us -> 76.9 us (0.966)
  local copies, waits for them, and re-layouts: 5.27 us -> 3.47 us
  Pallas kernels: 73 us -> 72.1 us
    transpose x2 -> x0, local copies, waits for them, and re-layouts: 1.12 us -> none  [on_device(): return out[:, :nz, :].transpose(1, 0, 2)]
    pallas_call x1, Pallas kernels: 73 us -> 72.1 us  [on_device(): pl.pallas_call(functools.partial(kernel, n_gx, n_gy, rows, depth), out_sh...]
    unnamed x9 -> x8, local copies, waits for them, and re-layouts: 3.35 us -> 2.79 us
where the time goes in v1:
time: 76.9 us; the launch traced here: 76.7 us
  Pallas kernels  72.1 us (94%)
  local copies, waits for them, and re-layouts  3.47 us (5%)
  other arithmetic  1 us (1%)
    pallas_call x1, Pallas kernels, on_device(): pl.pallas_call(functools.partial(kernel, n_gx, n_gy, rows, depth), out_sh...  72.1 us
    unnamed x8, local copies, waits for them, and re-layouts  2.79 us

profile of v1, /device:TPU:0, one launch (start us, length us, event | category | flops | bytes accessed | tf_op | source)
XLA Modules:
  0.0 76.7 jit_solution(7042656241102693398)
XLA Ops:
  0.0 0.1 pad.13.clone
  0.1 0.8 %slice_bitcast_fusion.1 = (f32[1,70]{1,0:T(1,128)S(1)}, f32[1,70]{1,0:T(1,128)S(1)}, f32[1,70]{1,0:T(1,128)S(1)}) fusion(f32[71]{0:T(128)} %param.7), kind=kLoop, calls=%fused_computation.12 | loop fusion | flops 140 | bytes 1400 | tf_op jit(solution)/shard_map/stack | solution.py:314
  0.9 0.1 broadcast_in_dim.4.kz_ref
  1.0 0.9 %copy.7 = f32[4,5,14,14]{3,2,1,0:T(8,128)S(1)} copy(f32[4,5,14,14]{3,0,2,1:T(4,128)} %param.8) | data formatting | bytes 31360 | tf_op args[3]
  1.9 0.1 mul.28
  2.0 0.1 mul.29
  2.1 0.1 mul.26
  2.2 0.0 copy-start
  2.2 0.0 copy-start.1
  2.2 0.0 copy-start.2
  2.3 0.2 mul.27
  2.6 0.1 maximum_maximum_fusion.binv_ref
  2.7 0.7 copy-done
  3.4 0.3 copy-done.1
  3.6 0.0 copy-done.2
  3.6 72.1 %shard_map.55 = f32[70,24,1,128]{3,2,1,0:T(1,128)S(1)} custom-call(s32[1,1,4]{2,1,0:T(1,128)S(1)} %copy-done.2, f32[70,24,1,128]{3,2,1,0:T(1,128)S(1)} %bitcast.10, f32[70,24,1,128]{3,2,1,0:T(1,128)S(1)} %bitcast.11, f32[3,72,128]{2,1,0:T(8,128)S(1)} %broadcast_in_dim.4.kz_ref, bf16[4,72,224]{2,1,0:T(8,128)(2,1)S(1)} %maximum_maximum_fusion.binv_ref), custom_call_target="tpu_custom_call" | custom-call | tf_op jit(solution)/shard_map/pallas_call | solution.py:328
  75.8 0.9 %copy.9 = f32[70,24,128]{2,1,0:T(8,128)} copy(f32[70,24,128]{2,1,0:T(8,128)S(1)} %bitcast.9) | data formatting | bytes 1720320
  (5 shorter events, 0.1 us)
Async XLA Ops:
  2.2 1.2 %copy-start = (f32[70,24,128]{2,1,0:T(8,128)S(1)}, f32[70,24,128]{2,1,0:T(8,128)}, u32[]{:S(2)}) copy-start(f32[70,24,128]{2,1,0:T(8,128)} %param.5) | copy-start | bytes 2580484
  2.2 1.4 %copy-start.1 = (f32[70,24,128]{2,1,0:T(8,128)S(1)}, f32[70,24,128]{2,1,0:T(8,128)}, u32[]{:S(2)}) copy-start(f32[70,24,128]{2,1,0:T(8,128)} %param.6) | copy-start | bytes 2580484
  2.2 1.4 %copy-start.2 = (s32[1,1,4]{2,1,0:T(1,128)S(1)}, s32[1,1,4]{2,1,0:T(1,128)}, u32[]{:S(2)}) copy-start(s32[1,1,4]{2,1,0:T(1,128)} %flip_ref.1) | copy-start | bytes 52

commit v2 on v1

--- a/solution.py
+++ b/solution.py
@@ -25,6 +25,12 @@
     both = jnp.concatenate([hi, lo], axis=0).astype(BF)
     out = jnp.dot(both, matrix, preferred_element_type=F32)
     return out[:depth] + out[depth:]
+
+
+def permute_many(tiles, matrix):
+    depth = tiles[0].shape[0]
+    out = permute(jnp.concatenate(tiles, axis=0), matrix)
+    return [out[depth * i:depth * (i + 1)] for i in range(len(tiles))]
 
 
 FOLD_ROW = (1, 2, 4, 4)
@@ -59,8 +65,8 @@
     return jnp.dot(binv, cat, preferred_element_type=F32)
 
 
-def kernel(n_gx, n_gy, rows0, depth, flip_ref, s_in, c_in, kz_ref, binv_ref, out_ref,
-           stage_s, stage_c, row_send, io_sem,
+def kernel(n_gx, n_gy, rows0, depth, flip_ref, s_in, c_in, vert_ref, inv_ref, out_ref,
+           stage_s, stage_c, row_send, kz_ref, base, binv_ref, io_sem,
            va0, va1, va2, va3, vb0, vb1, vb2, vb3, s0, s1, s2, s3, d0, d1, d2, d3,
            edge, held, px, py, resm, prom, send_sem, recv_sem):
     va, vb = (va0, va1, va2, va3), (vb0, vb1, vb2, vb3)
@@ -72,11 +78,11 @@
         (gx, lax.rem(gy + n_gy - 1, n_gy)),
         (gx, lax.rem(gy + 1, n_gy)),
     )
-    loads = []
-    for x in range(rows0):
-        loads.append(pltpu.make_async_copy(s_in.at[:, x, 0, :], stage_s.at[x], io_sem.at[0, x]))
-        loads.append(pltpu.make_async_copy(c_in.at[:, x, 0, :], stage_c.at[x], io_sem.at[1, x]))
-    for load in loads:
+    load_s = [pltpu.make_async_copy(s_in.at[:, x, 0, :], stage_s.at[x], io_sem.at[0, x])
+              for x in range(rows0)]
+    load_c = [pltpu.make_async_copy(c_in.at[:, x, 0, :], stage_c.at[x], io_sem.at[1, x])
+              for x in range(rows0)]
+    for load in load_s + load_c:
         load.start()
     barrier = pltpu.get_barrier_semaphore()
     for peer in peers:
@@ -87,6 +93,32 @@
     lane = lax.broadcasted_iota(jnp.int32, (depth, LANES), 1)
     ki = lax.broadcasted_iota(jnp.int32, (LANES, LANES), 0)
     mi = lax.broadcasted_iota(jnp.int32, (LANES, LANES), 1)
+    level_z = lax.broadcasted_iota(jnp.int32, (depth, LANES), 0)
+    nz = stage_s.shape[1]
+    coef = jnp.broadcast_to(vert_ref[...], (depth, LANES))
+
+    def down_lanes(shift):
+        hit = (lane == level_z + shift) & (level_z < nz)
+        return jnp.broadcast_to(jnp.sum(jnp.where(hit, coef, 0.0), axis=1, keepdims=True), (depth, LANES))
+
+    up, down = down_lanes(1), down_lanes(0)
+    kz_ref[0] = up
+    kz_ref[1] = down
+    kz_ref[2] = jnp.where(level_z < nz, 4.0 + up + down, 0.0)
+    nblk, blk = inv_ref.shape[0], inv_ref.shape[1]
+    for l in range(LEVELS):
+        base[l] = jnp.zeros((depth, LANES), F32)
+        for k in range(nblk):
+            base[l, blk * k:blk * (k + 1), 0:blk] = inv_ref[k, :, l, :] * 0.0625
+        block = base[l]
+        full = block
+        for k in range(1, nblk):
+            full = jnp.where(level_z >= blk * k, pltpu.roll(block, blk * k, 1), full)
+        hi, lo = split2(full)
+        turned = pltpu.roll(hi, depth, 1)
+        first = jnp.where(lane < depth, hi, turned)
+        second = jnp.where(lane < 2 * depth - LANES, turned, pltpu.roll(lo, 2 * depth - LANES, 1))
+        binv_ref[l] = jnp.concatenate([first, second], axis=1).astype(BF)
     flips = [flip_ref[0, 0, s] > 0 for s in range(4)]
 
     def as_matrix(hit, value=1.0):
@@ -117,14 +149,21 @@
             buf[0] = jnp.zeros((depth, LANES), F32)
             buf[nrow[l] + 1] = jnp.zeros((depth, LANES), F32)
 
-    group = [4, 4, 6, 3]
+    group = [4, 4, 3, 3]
+    per_step = [8, 12, 6, 3]
 
     def each_group(l, body, carry=0):
         g = group[l] if nrow[l] % group[l] == 0 else 1
-        trips = nrow[l] // g
-        if trips == 1:
-            return body(0, g, carry)
-        return lax.fori_loop(0, trips, lambda i, acc: body(i * g, g, acc), carry)
+        step = per_step[l] if nrow[l] % per_step[l] == 0 else g
+
+        def run(x0, acc):
+            for off in range(0, step, g):
+                acc = body(x0 + off, g, acc)
+            return acc
+
+        if step == nrow[l]:
+            return run(0, carry)
+        return lax.fori_loop(0, nrow[l] // step, lambda i, acc: run(i * step, acc), carry)
 
     def extract(acc, row, x, c):
         turned = pltpu.roll(row, 2 * x + 1, 1)
@@ -166,15 +205,13 @@
             copies[-1].start()
         return copies
 
-    up, down = kz_ref[0], kz_ref[1]
-
     def partial(l, v, x):
         c = ncol[l]
         mid = v[x + 1]
         r = src[l][x] - dia[l][x] * mid + (v[x] + v[x + 2])
         r = r + jnp.where(lane == 0, 0.0, pltpu.roll(mid, 1, 1))
         r = r + jnp.where(lane == c - 1, 0.0, pltpu.roll(mid, LANES - 1, 1))
-        r = r + up * pltpu.roll(mid, depth - 1, 0) + down * pltpu.roll(mid, 1, 0)
+        r = r + kz_ref[0] * pltpu.roll(mid, depth - 1, 0) + kz_ref[1] * pltpu.roll(mid, 1, 0)
         return r, mid
 
     def halos(k, l):
@@ -189,10 +226,39 @@
 
     count = [0]
 
+    tail = jnp.zeros((depth - nz, LANES), F32)
+
+    def first_field(v):
+        acc = jnp.zeros((depth, LANES), F32)
+        g = 4 if rows0 % 4 == 0 else 1
+        for x0 in range(0, rows0, g):
+            rows = []
+            for x in range(x0, x0 + g):
+                load_s[x].wait()
+                rows.append(jnp.concatenate([stage_s[x] * 16.0, tail], axis=0))
+                src[0][x] = rows[-1]
+            d = block_dot(binv_ref[0, :, 0:3 * depth + 8], jnp.concatenate(rows, axis=1))
+            for j in range(g):
+                row = d[:, j * LANES:(j + 1) * LANES]
+                v[x0 + j + 1] = row
+                acc = extract(acc, row, x0 + j, ncol[0])
+        put_ends(0, acc)
+
+    def take_coef():
+        for x in range(rows0):
+            load_c[x].wait()
+            dia[0][x] = jnp.concatenate([stage_c[x], tail], axis=0) + kz_ref[2]
+
+    def coarse_coef():
+        for l in range(LEVELS - 1):
+            pairs = [dia[l][2 * x] + dia[l][2 * x + 1] for x in range(nrow[l + 1])]
+            for x, row in enumerate(permute_many(pairs, resm[l])):
+                dia[l + 1][x] = row
+
     def from_zero(l, v):
         def body(x0, g, acc):
             rr = jnp.concatenate([src[l][x0 + j] for j in range(g)], axis=1)
-            d = block_dot(binv_ref[l], rr)
+            d = block_dot(binv_ref[l, :, 0:3 * depth + 8], rr)
             for j in range(g):
                 row = d[:, j * LANES:(j + 1) * LANES]
                 v[x0 + j + 1] = row
@@ -200,15 +266,17 @@
             return acc
         put_ends(l, each_group(l, body, jnp.zeros((depth, LANES), F32)))
 
-    def relax(l, v, w, pending=None):
+    def relax(l, v, w, pending=None, start=False):
         k = count[0]
         count[0] += 1
         copies = send(k, l, v)
         settle(l, v, pending)
+        if start:
+            take_coef()
 
         def body(x0, g, acc):
             parts = [partial(l, v, x0 + j) for j in range(g)]
-            d = block_dot(binv_ref[l], jnp.concatenate([p[0] for p in parts], axis=1))
+            d = block_dot(binv_ref[l, :, 0:3 * depth + 8], jnp.concatenate([p[0] for p in parts], axis=1))
             for j in range(g):
                 row = parts[j][1] + d[:, j * LANES:(j + 1) * LANES]
                 w[x0 + j + 1] = row
@@ -216,10 +284,12 @@
             return acc
 
         acc = each_group(l, body, jnp.zeros((depth, LANES), F32))
+        if start:
+            coarse_coef()
         for copy in copies:
             copy.wait()
         r, c = nrow[l], ncol[l]
-        corr = block_dot(binv_ref[l], jnp.concatenate(halos(k, l), axis=1))
+        corr = block_dot(binv_ref[l, :, 0:3 * depth + 8], jnp.concatenate(halos(k, l), axis=1))
         low, high, beside = (corr[:, j * LANES:(j + 1) * LANES] for j in range(3))
         w[1] = w[1] + low + insert(beside, 0, c)
         w[r] = w[r] + high + insert(beside, r - 1, c)
@@ -254,14 +324,15 @@
         low, high, beside = halos(k, l)
         w[1] = w[1] + low
         w[r] = w[r] + high
-        for x in range(0, r, 2):
-            pair = w[x + 1] + w[x + 2] + insert(beside, x, c) + insert(beside, x + 1, c)
-            src[l + 1][x // 2] = permute(pair, resm[l])
+        pairs = [w[x + 1] + w[x + 2] + insert(beside, x, c) + insert(beside, x + 1, c)
+                 for x in range(0, r, 2)]
+        for x, row in enumerate(permute_many(pairs, resm[l])):
+            src[l + 1][x] = row
 
     def add_coarse(l, v, coarse):
         acc = jnp.zeros((depth, LANES), F32)
-        for x in range(nrow[l + 1]):
-            fine = permute(coarse[x + 1], prom[l])
+        spread = permute_many([coarse[x + 1] for x in range(nrow[l + 1])], prom[l])
+        for x, fine in enumerate(spread):
             for j in (2 * x, 2 * x + 1):
                 row = v[j + 1] + fine
                 v[j + 1] = row
@@ -270,14 +341,18 @@
 
     def cycle(l):
         a, b = va[l], vb[l]
-        from_zero(l, a)
+        if l == 0:
+            first_field(a)
+            pl.semaphore_wait(barrier, 4)
+        else:
+            from_zero(l, a)
         if l == LEVELS - 1:
             p = relax(l, a, b)
             p = relax(l, b, a, p)
             p = relax(l, a, b, p)
             settle(l, b, p)
             return b
-        p = relax(l, a, b)
+        p = relax(l, a, b, start=l == 0)
         residual(l, b, a, p)
         add_coarse(l, b, cycle(l + 1))
         p = relax(l, b, a)
@@ -285,17 +360,6 @@
         settle(l, b, p)
         return b
 
-    for load in loads:
-        load.wait()
-    nz = stage_s.shape[1]
-    tail = jnp.zeros((depth - nz, LANES), F32)
-    for x in range(rows0):
-        src[0][x] = jnp.concatenate([stage_s[x] * 16.0, tail], axis=0)
-        dia[0][x] = jnp.concatenate([stage_c[x], tail], axis=0) + kz_ref[2]
-    for l in range(LEVELS - 1):
-        for x in range(nrow[l + 1]):
-            dia[l + 1][x] = permute(dia[l][2 * x] + dia[l][2 * x + 1], resm[l])
-    pl.semaphore_wait(barrier, 4)
     v = cycle(0)
     stores = []
     for x in range(rows0):
@@ -309,16 +373,9 @@
 def on_device(n_gx, n_gy, right_side, helm_coef, vert_coef, block_inverse, edge_flip):
     nz, rows, cols = right_side.shape
     depth = -(-nz // 8) * 8
-    pad = depth - nz
     s, c = (a.reshape(nz, rows, 1, cols) for a in (right_side, helm_coef))
-    kz = jnp.stack([vert_coef[1:], vert_coef[:-1], 4.0 + vert_coef[1:] + vert_coef[:-1]])
-    kz = jnp.broadcast_to(jnp.pad(kz, ((0, 0), (0, pad)))[:, :, None], (3, depth, LANES))
-    nblk = nz // BLK
-    eye = jnp.eye(nblk, dtype=F32)[None, :, None, :, None]
-    full = (block_inverse[:, :, :, None, :] * eye).reshape(LEVELS, nz, nz) * 0.0625
-    full = jnp.pad(full, ((0, 0), (0, pad), (0, pad)))
-    hi = lax.reduce_precision(full, 8, 7)
-    binv = jnp.concatenate([hi, hi, full - hi, jnp.zeros((LEVELS, depth, 8), F32)], axis=2).astype(BF)
+    vert = jnp.pad(vert_coef, (0, LANES - nz - 1)).reshape(1, LANES)
+    inv = block_inverse.transpose(1, 2, 0, 3)
 
     tile = lambda r: pltpu.VMEM((r, depth, LANES), F32)
     rl = [rows >> l for l in range(LEVELS)]
@@ -334,6 +391,9 @@
             pltpu.VMEM((rows, nz, LANES), F32),
             pltpu.VMEM((rows, nz, LANES), F32),
             pltpu.VMEM((2, depth, LANES), F32),
+            pltpu.VMEM((3, depth, LANES), F32),
+            pltpu.VMEM((LEVELS, depth, LANES), F32),
+            pltpu.VMEM((LEVELS, depth, 2 * LANES), BF),
             pltpu.SemaphoreType.DMA((2, rows)),
         ] + [tile(r + 2) for r in rl] * 2 + [tile(r) for r in rl] * 2 + [
             pltpu.VMEM((depth, LANES), F32),
@@ -346,8 +406,8 @@
             pltpu.SemaphoreType.DMA((steps, 4)),
         ],
         compiler_params=pltpu.CompilerParams(
-            collective_id=0, has_side_effects=True, vmem_limit_bytes=40 * 1024 * 1024),
-    )(edge_flip, s, c, kz, binv)
+            collective_id=0, has_side_effects=True, vmem_limit_bytes=60 * 1024 * 1024),
+    )(edge_flip, s, c, vert, inv)
     return out.reshape(nz, rows, cols)
 
 

time: 76.9 us -> 73.2 us (0.952)
  Pallas kernels: 72.1 us -> 69.7 us
  other arithmetic: 1 us -> 0 us
    pallas_call x1, Pallas kernels: 72.1 us -> 69.7 us  [on_device(): pl.pallas_call(functools.partial(kernel, n_gx, n_gy, rows, depth), out_sh...]
    another operation x3 -> x0, other arithmetic: 0.85 us -> none  [the longest x2 0.81 us: on_device(): jnp.stack([vert_coef[1:], vert_coef[:-1], 4.0 + vert_coef[1:] + vert_coef...]
    unnamed x8 -> x3, local copies, waits for them, and re-layouts: 2.79 us -> 2.77 us
where the time goes in v2:
time: 73.2 us; the launch traced here: 73 us
  Pallas kernels  69.7 us (95%)
  local copies, waits for them, and re-layouts  3.29 us (4%)
    pallas_call x1, Pallas kernels, on_device(): pl.pallas_call(functools.partial(kernel, n_gx, n_gy, rows, depth), out_sh...  69.7 us
    unnamed x3, local copies, waits for them, and re-layouts  2.77 us

profile of v2, /device:TPU:0, one launch (start us, length us, event | category | flops | bytes accessed | tf_op | source)
XLA Modules:
  0.0 73.0 jit_solution(785998006822477204)
XLA Ops:
  0.0 0.0 copy-start
  0.0 0.7 copy-done
  0.7 0.5 pad_bitcast_fusion.vert_ref
  1.2 69.7 %shard_map.55 = f32[70,24,1,128]{3,2,1,0:T(1,128)} custom-call(s32[1,1,4]{2,1,0:T(1,128)} %flip_ref.1, f32[70,24,1,128]{3,2,1,0:T(1,128)} %bitcast.7, f32[70,24,1,128]{3,2,1,0:T(1,128)} %bitcast.8, f32[1,128]{1,0:T(1,128)} %pad_bitcast_fusion.vert_ref, f32[5,14,4,14]{3,2,1,0:T(4,128)} %bitcast.9), custom_call_target="tpu_custom_call" | custom-call | tf_op jit(solution)/shard_map/pallas_call | solution.py:385
  70.9 2.1 %copy.7 = f32[70,24,128]{2,1,0:T(8,128)} copy(f32[70,24,128]{2,1,0:T(8,128)} %bitcast.6) | data formatting | bytes 1720320
Async XLA Ops:
  0.0 0.7 copy-start

commit v3 on v2

--- a/solution.py
+++ b/solution.py
@@ -19,18 +19,8 @@
     return hi, x - hi
 
 
-def permute(x, matrix):
-    depth = x.shape[0]
-    hi, lo = split2(x)
-    both = jnp.concatenate([hi, lo], axis=0).astype(BF)
-    out = jnp.dot(both, matrix, preferred_element_type=F32)
-    return out[:depth] + out[depth:]
-
-
-def permute_many(tiles, matrix):
-    depth = tiles[0].shape[0]
-    out = permute(jnp.concatenate(tiles, axis=0), matrix)
-    return [out[depth * i:depth * (i + 1)] for i in range(len(tiles))]
+def take(tile, spot):
+    return jnp.take_along_axis(tile, spot, axis=1, mode="promise_in_bounds")
 
 
 FOLD_ROW = (1, 2, 4, 4)
@@ -50,12 +40,12 @@
     return jnp.concatenate(outs, axis=0)
 
 
-def unpack(packed, matrix, depth, fold):
-    wide = permute(packed, matrix)
+def unpack(packed, spot, keep, depth, fold):
     parts = []
     for unit in range(depth // 8):
         j, q = divmod(unit, fold)
-        parts.append(wide[8 * j:8 * j + 8, LANES * q:LANES * (q + 1)])
+        at = (spot + q * (LANES // fold)) & (LANES - 1)
+        parts.append(jnp.where(keep, take(packed[8 * j:8 * j + 8], at), 0.0))
     return jnp.concatenate(parts, axis=0)
 
 
@@ -68,7 +58,7 @@
 def kernel(n_gx, n_gy, rows0, depth, flip_ref, s_in, c_in, vert_ref, inv_ref, out_ref,
            stage_s, stage_c, row_send, kz_ref, base, binv_ref, io_sem,
            va0, va1, va2, va3, vb0, vb1, vb2, vb3, s0, s1, s2, s3, d0, d1, d2, d3,
-           edge, held, px, py, resm, prom, send_sem, recv_sem):
+           edge, held, send_sem, recv_sem):
     va, vb = (va0, va1, va2, va3), (vb0, vb1, vb2, vb3)
     src, dia = (s0, s1, s2, s3), (d0, d1, d2, d3)
     gx, gy = lax.axis_index("gx"), lax.axis_index("gy")
@@ -91,11 +81,10 @@
     nrow = [rows0 >> l for l in range(LEVELS)]
     ncol = [LANES >> l for l in range(LEVELS)]
     lane = lax.broadcasted_iota(jnp.int32, (depth, LANES), 1)
-    ki = lax.broadcasted_iota(jnp.int32, (LANES, LANES), 0)
-    mi = lax.broadcasted_iota(jnp.int32, (LANES, LANES), 1)
     level_z = lax.broadcasted_iota(jnp.int32, (depth, LANES), 0)
     nz = stage_s.shape[1]
-    coef = jnp.broadcast_to(vert_ref[...], (depth, LANES))
+    coef = jnp.concatenate([vert_ref[...], jnp.zeros((1, LANES - nz - 1), F32)], axis=1)
+    coef = jnp.broadcast_to(coef, (depth, LANES))
 
     def down_lanes(shift):
         hit = (lane == level_z + shift) & (level_z < nz)
@@ -121,28 +110,11 @@
         binv_ref[l] = jnp.concatenate([first, second], axis=1).astype(BF)
     flips = [flip_ref[0, 0, s] > 0 for s in range(4)]
 
-    def as_matrix(hit, value=1.0):
-        return jnp.where(hit, value, 0.0).astype(F32).astype(BF)
-
-    for l in range(LEVELS):
-        r, c = nrow[l], ncol[l]
-        for side in range(2):
-            spot = jnp.where(flips[side], c - 1 - mi, mi)
-            for q in range(FOLD_ROW[l]):
-                px[l, side, :, LANES * q:LANES * (q + 1)] = as_matrix(
-                    (ki == spot + q * (LANES // FOLD_ROW[l])) & (mi < c))
-        xm = mi >> 1
-        xh = ((mi - c) & (LANES - 1)) >> 1
-        for q in range(FOLD_END[l]):
-            at = q * (LANES // FOLD_END[l])
-            cols = slice(LANES * q, LANES * (q + 1))
-            from_low = (2 * jnp.where(flips[2], r - 1 - xm, xm) + c + at) & (LANES - 1)
-            py[l, 0:LANES, cols] = as_matrix((ki == from_low) & ((mi & 1) == 1) & (xm < r))
-            from_high = (2 * jnp.where(flips[3], r - 1 - xh, xh) + 1 + at) & (LANES - 1)
-            py[l, LANES:, cols] = as_matrix((ki == from_high) & ((mi & 1) == 0) & (xh < r))
-    for l in range(LEVELS - 1):
-        resm[l] = as_matrix(((ki >> 1) == mi) & (mi < ncol[l + 1]), 0.25)
-        prom[l] = as_matrix(((mi >> 1) == ki) & (mi < ncol[l]))
+    lane8 = lax.broadcasted_iota(jnp.int32, (8, LANES), 1)
+
+    def restrict(row, l):
+        both = row + pltpu.roll(row, LANES - 1, 1)
+        return jnp.where(lane < ncol[l + 1], take(both, (2 * lane) & (LANES - 1)) * 0.25, 0.0)
 
     for l in range(LEVELS):
         for buf in (va[l], vb[l]):
@@ -215,13 +187,21 @@
         return r, mid
 
     def halos(k, l):
+        r, c = nrow[l], ncol[l]
         size = row_size(l)
         low, high = (
-            unpack(held[k, side, 0:size], px[l, side, :, 0:LANES * FOLD_ROW[l]], depth, FOLD_ROW[l])
+            unpack(held[k, side, 0:size], jnp.where(flips[side], c - 1 - lane8, lane8), lane8 < c,
+                   depth, FOLD_ROW[l])
             for side in range(2))
         size = end_size(l)
-        both = jnp.concatenate([held[k, 2, 0:size], held[k, 3, 0:size]], axis=1)
-        beside = unpack(both, py[l, :, 0:LANES * FOLD_END[l]], depth, FOLD_END[l])
+        odd = (lane8 & 1) == 1
+        xm = lane8 >> 1
+        xh = ((lane8 - c) & (LANES - 1)) >> 1
+        from_low = 2 * jnp.where(flips[2], r - 1 - xm, xm) + c
+        from_high = 2 * jnp.where(flips[3], r - 1 - xh, xh) + 1
+        keep = jnp.where(odd, xm, xh) < r
+        both = jnp.where((lane[0:size] & 1) == 1, held[k, 3, 0:size], held[k, 2, 0:size])
+        beside = unpack(both, jnp.where(odd, from_low, from_high), keep, depth, FOLD_END[l])
         return low, high, beside
 
     count = [0]
@@ -251,9 +231,8 @@
 
     def coarse_coef():
         for l in range(LEVELS - 1):
-            pairs = [dia[l][2 * x] + dia[l][2 * x + 1] for x in range(nrow[l + 1])]
-            for x, row in enumerate(permute_many(pairs, resm[l])):
-                dia[l + 1][x] = row
+            for x in range(nrow[l + 1]):
+                dia[l + 1][x] = restrict(dia[l][2 * x] + dia[l][2 * x + 1], l)
 
     def from_zero(l, v):
         def body(x0, g, acc):
@@ -324,15 +303,14 @@
         low, high, beside = halos(k, l)
         w[1] = w[1] + low
         w[r] = w[r] + high
-        pairs = [w[x + 1] + w[x + 2] + insert(beside, x, c) + insert(beside, x + 1, c)
-                 for x in range(0, r, 2)]
-        for x, row in enumerate(permute_many(pairs, resm[l])):
-            src[l + 1][x] = row
+        for x in range(0, r, 2):
+            pair = w[x + 1] + w[x + 2] + insert(beside, x, c) + insert(beside, x + 1, c)
+            src[l + 1][x // 2] = restrict(pair, l)
 
     def add_coarse(l, v, coarse):
         acc = jnp.zeros((depth, LANES), F32)
-        spread = permute_many([coarse[x + 1] for x in range(nrow[l + 1])], prom[l])
-        for x, fine in enumerate(spread):
+        for x in range(nrow[l + 1]):
+            fine = take(coarse[x + 1], lane >> 1)
             for j in (2 * x, 2 * x + 1):
                 row = v[j + 1] + fine
                 v[j + 1] = row
@@ -374,18 +352,19 @@
     nz, rows, cols = right_side.shape
     depth = -(-nz // 8) * 8
     s, c = (a.reshape(nz, rows, 1, cols) for a in (right_side, helm_coef))
-    vert = jnp.pad(vert_coef, (0, LANES - nz - 1)).reshape(1, LANES)
+    vert = vert_coef.reshape(1, nz + 1)
     inv = block_inverse.transpose(1, 2, 0, 3)
 
     tile = lambda r: pltpu.VMEM((r, depth, LANES), F32)
     rl = [rows >> l for l in range(LEVELS)]
     steps = 4 * (LEVELS - 1) + 3
     hbm = pl.BlockSpec(memory_space=pl.ANY)
+    far = pl.BlockSpec(memory_space=pltpu.HBM)
     vm = pl.BlockSpec(memory_space=pltpu.VMEM)
     out = pl.pallas_call(
         functools.partial(kernel, n_gx, n_gy, rows, depth),
         out_shape=jax.ShapeDtypeStruct((nz, rows, 1, LANES), F32),
-        in_specs=[pl.BlockSpec(memory_space=pltpu.SMEM), hbm, hbm, vm, vm],
+        in_specs=[pl.BlockSpec(memory_space=pltpu.SMEM), far, far, vm, vm],
         out_specs=hbm,
         scratch_shapes=[
             pltpu.VMEM((rows, nz, LANES), F32),
@@ -398,15 +377,11 @@
         ] + [tile(r + 2) for r in rl] * 2 + [tile(r) for r in rl] * 2 + [
             pltpu.VMEM((depth, LANES), F32),
             pltpu.VMEM((steps, 4, depth, LANES), F32),
-            pltpu.VMEM((LEVELS, 2, LANES, LANES * max(FOLD_ROW)), BF),
-            pltpu.VMEM((LEVELS, 2 * LANES, LANES * max(FOLD_END)), BF),
-            pltpu.VMEM((LEVELS - 1, LANES, LANES), BF),
-            pltpu.VMEM((LEVELS - 1, LANES, LANES), BF),
             pltpu.SemaphoreType.DMA((steps, 4)),
             pltpu.SemaphoreType.DMA((steps, 4)),
         ],
         compiler_params=pltpu.CompilerParams(
-            collective_id=0, has_side_effects=True, vmem_limit_bytes=60 * 1024 * 1024),
+            collective_id=0, has_side_effects=True, vmem_limit_bytes=40 * 1024 * 1024),
     )(edge_flip, s, c, vert, inv)
     return out.reshape(nz, rows, cols)
 

time: 73.2 us -> 74.6 us (1.019)
  local copies, waits for them, and re-layouts: 3.29 us -> 4.8 us
    unnamed x3 -> x11, local copies, waits for them, and re-layouts: 2.77 us -> 4.8 us
where the time goes in v3:
time: 74.6 us; the launch traced here: 74.3 us
  Pallas kernels  69.5 us (93%)
  local copies, waits for them, and re-layouts  4.8 us (6%)
    pallas_call x1, Pallas kernels, on_device(): pl.pallas_call(functools.partial(kernel, n_gx, n_gy, rows, depth), out_sh...  69.5 us
    unnamed x11, local copies, waits for them, and re-layouts  4.8 us

profile of v3, /device:TPU:0, one launch (start us, length us, event | category | flops | bytes accessed | tf_op | source)
XLA Modules:
  0.0 74.3 jit_solution(17341614699029034877)
XLA Ops:
  0.0 0.0 copy-start.3
  0.0 0.0 copy-start.4
  0.0 0.7 copy-done.3
  0.7 0.0 copy-done.4
  0.7 0.0 copy-start
  0.7 1.2 %copy-done = f32[70,24,128]{2,1,0:T(8,128)S(1)} copy-done((f32[70,24,128]{2,1,0:T(8,128)S(1)}, f32[70,24,128]{2,1,0:T(8,128)}, u32[]{:S(2)}) %copy-start) | copy-done | bytes 860184
  1.8 0.0 copy-start.1
  1.8 1.2 %copy-done.1 = f32[70,24,128]{2,1,0:T(8,128)S(1)} copy-done((f32[70,24,128]{2,1,0:T(8,128)S(1)}, f32[70,24,128]{2,1,0:T(8,128)}, u32[]{:S(2)}) %copy-start.1) | copy-done | bytes 860184
  3.0 0.0 copy-start.2
  3.0 0.9 %copy-done.2 = f32[4,5,14,14]{3,0,2,1:T(4,128)S(1)} copy-done((f32[4,5,14,14]{3,0,2,1:T(4,128)S(1)}, f32[4,5,14,14]{3,0,2,1:T(4,128)}, u32[]{:S(2)}) %copy-start.2) | copy-done | bytes 15704
  3.9 69.5 %shard_map.55 = f32[70,24,1,128]{3,2,1,0:T(1,128)S(1)} custom-call(s32[1,1,4]{2,1,0:T(1,128)S(1)} %copy-done.3, f32[70,24,1,128]{3,2,1,0:T(1,128)S(1)} %bitcast.6, f32[70,24,1,128]{3,2,1,0:T(1,128)S(1)} %bitcast.7, f32[1,71]{1,0:T(1,128)S(1)} %bitcast.9, f32[5,14,4,14]{3,2,1,0:T(4,128)S(1)} %bitcast.8), custom_call_target="tpu_custom_call" | custom-call | tf_op jit(solution)/shard_map/pallas_call | solution.py:364
  73.4 0.9 %copy.7 = f32[70,24,128]{2,1,0:T(8,128)} copy(f32[70,24,128]{2,1,0:T(8,128)S(1)} %bitcast.5) | data formatting | bytes 1720320
Async XLA Ops:
  0.0 0.7 copy-start.3
  0.0 0.7 copy-start.4
  0.7 1.2 %copy-start = (f32[70,24,128]{2,1,0:T(8,128)S(1)}, f32[70,24,128]{2,1,0:T(8,128)}, u32[]{:S(2)}) copy-start(f32[70,24,128]{2,1,0:T(8,128)} %param.5) | copy-start | bytes 2580484
  1.8 1.2 %copy-start.1 = (f32[70,24,128]{2,1,0:T(8,128)S(1)}, f32[70,24,128]{2,1,0:T(8,128)}, u32[]{:S(2)}) copy-start(f32[70,24,128]{2,1,0:T(8,128)} %param.6) | copy-start | bytes 2580484
  3.0 0.9 %copy-start.2 = (f32[4,5,14,14]{3,0,2,1:T(4,128)S(1)}, f32[4,5,14,14]{3,0,2,1:T(4,128)}, u32[]{:S(2)}) copy-start(f32[4,5,14,14]{3,0,2,1:T(4,128)} %param.8) | copy-start | bytes 47044

commit v4 on v3

--- a/solution.py
+++ b/solution.py
@@ -137,6 +137,19 @@
             return run(0, carry)
         return lax.fori_loop(0, nrow[l] // step, lambda i, acc: run(i * step, acc), carry)
 
+    def row_loop(n, step, body, carry=0):
+        if n <= step or n % step:
+            for i in range(n):
+                carry = body(i, carry)
+            return carry
+
+        def run(t, acc):
+            for j in range(step):
+                acc = body(t * step + j, acc)
+            return acc
+
+        return lax.fori_loop(0, n // step, run, carry)
+
     def extract(acc, row, x, c):
         turned = pltpu.roll(row, 2 * x + 1, 1)
         hit = (lane == 2 * x + 1) | (lane == ((2 * x + c) & (LANES - 1)))
@@ -282,8 +295,12 @@
         if beside is None:
             return
         c = ncol[l]
-        for x in range(1, nrow[l] - 1):
-            v[x + 1] = v[x + 1] + insert(beside, x, c)
+
+        def body(i, acc):
+            v[i + 2] = v[i + 2] + insert(beside, i + 1, c)
+            return acc
+
+        row_loop(nrow[l] - 2, 2 if nrow[l] > 6 else nrow[l], body)
 
     def residual(l, v, w, pending):
         k = count[0]
@@ -303,19 +320,25 @@
         low, high, beside = halos(k, l)
         w[1] = w[1] + low
         w[r] = w[r] + high
-        for x in range(0, r, 2):
+
+        def fold(i, acc):
+            x = 2 * i
             pair = w[x + 1] + w[x + 2] + insert(beside, x, c) + insert(beside, x + 1, c)
-            src[l + 1][x // 2] = restrict(pair, l)
+            src[l + 1][i] = restrict(pair, l)
+            return acc
+
+        row_loop(r // 2, 3, fold)
 
     def add_coarse(l, v, coarse):
-        acc = jnp.zeros((depth, LANES), F32)
-        for x in range(nrow[l + 1]):
+        def body(x, acc):
             fine = take(coarse[x + 1], lane >> 1)
             for j in (2 * x, 2 * x + 1):
                 row = v[j + 1] + fine
                 v[j + 1] = row
                 acc = extract(acc, row, j, ncol[l])
-        put_ends(l, acc)
+            return acc
+
+        put_ends(l, row_loop(nrow[l + 1], 3, body, jnp.zeros((depth, LANES), F32)))
 
     def cycle(l):
         a, b = va[l], vb[l]
@@ -359,12 +382,11 @@
     rl = [rows >> l for l in range(LEVELS)]
     steps = 4 * (LEVELS - 1) + 3
     hbm = pl.BlockSpec(memory_space=pl.ANY)
-    far = pl.BlockSpec(memory_space=pltpu.HBM)
     vm = pl.BlockSpec(memory_space=pltpu.VMEM)
     out = pl.pallas_call(
         functools.partial(kernel, n_gx, n_gy, rows, depth),
         out_shape=jax.ShapeDtypeStruct((nz, rows, 1, LANES), F32),
-        in_specs=[pl.BlockSpec(memory_space=pltpu.SMEM), far, far, vm, vm],
+        in_specs=[pl.BlockSpec(memory_space=pltpu.SMEM), hbm, hbm, vm, vm],
         out_specs=hbm,
         scratch_shapes=[
             pltpu.VMEM((rows, nz, LANES), F32),
@@ -381,7 +403,7 @@
             pltpu.SemaphoreType.DMA((steps, 4)),
         ],
         compiler_params=pltpu.CompilerParams(
-            collective_id=0, has_side_effects=True, vmem_limit_bytes=40 * 1024 * 1024),
+            collective_id=0, has_side_effects=True, vmem_limit_bytes=60 * 1024 * 1024),
     )(edge_flip, s, c, vert, inv)
     return out.reshape(nz, rows, cols)
 

time: 74.6 us -> 73 us (0.979)
  local copies, waits for them, and re-layouts: 4.8 us -> 2.12 us
  Pallas kernels: 69.5 us -> 70.6 us
    unnamed x11 -> x1, local copies, waits for them, and re-layouts: 4.8 us -> 2.12 us
    pallas_call x1, Pallas kernels: 69.5 us -> 70.6 us  [on_device(): pl.pallas_call(functools.partial(kernel, n_gx, n_gy, rows, depth), out_sh...]
where the time goes in v4:
time: 73 us; the launch traced here: 72.7 us
  Pallas kernels  70.6 us (97%)
  local copies, waits for them, and re-layouts  2.12 us (3%)
    pallas_call x1, Pallas kernels, on_device(): pl.pallas_call(functools.partial(kernel, n_gx, n_gy, rows, depth), out_sh...  70.6 us
    unnamed x1, local copies, waits for them, and re-layouts  2.12 us

profile of v4, /device:TPU:0, one launch (start us, length us, event | category | flops | bytes accessed | tf_op | source)
XLA Modules:
  0.0 72.7 jit_solution(11212042547841454306)
XLA Ops:
  0.0 70.6 %shard_map.55 = f32[70,24,1,128]{3,2,1,0:T(1,128)} custom-call(s32[1,1,4]{2,1,0:T(1,128)} %flip_ref.1, f32[70,24,1,128]{3,2,1,0:T(1,128)} %bitcast.6, f32[70,24,1,128]{3,2,1,0:T(1,128)} %bitcast.7, f32[1,71]{1,0:T(1,128)} %bitcast.9, f32[5,14,4,14]{3,2,1,0:T(4,128)} %bitcast.8), custom_call_target="tpu_custom_call" | custom-call | tf_op jit(solution)/shard_map/pallas_call | solution.py:386
  70.6 2.1 %copy.7 = f32[70,24,128]{2,1,0:T(8,128)} copy(f32[70,24,128]{2,1,0:T(8,128)} %bitcast.5) | data formatting | bytes 1720320

commit v5 on v4

--- a/solution.py
+++ b/solution.py
@@ -137,18 +137,10 @@
             return run(0, carry)
         return lax.fori_loop(0, nrow[l] // step, lambda i, acc: run(i * step, acc), carry)
 
-    def row_loop(n, step, body, carry=0):
-        if n <= step or n % step:
-            for i in range(n):
-                carry = body(i, carry)
-            return carry
-
-        def run(t, acc):
-            for j in range(step):
-                acc = body(t * step + j, acc)
-            return acc
-
-        return lax.fori_loop(0, n // step, run, carry)
+    def row_loop(n, body, carry=0):
+        for i in range(n):
+            carry = body(i, carry)
+        return carry
 
     def extract(acc, row, x, c):
         turned = pltpu.roll(row, 2 * x + 1, 1)
@@ -161,6 +153,9 @@
     def insert(tile, x, c):
         return jnp.where(ends(c), pltpu.roll(tile, (LANES - 1) - 2 * x, 1), 0.0)
 
+    count = [0]
+    leaving = []
+
     def row_size(l):
         return 8 * -(-(depth // 8) // FOLD_ROW[l])
 
@@ -168,7 +163,7 @@
         return 8 * -(-(depth // 8) // FOLD_END[l])
 
     def put_ends(l, tile):
-        edge[0:end_size(l)] = pack(tile, FOLD_END[l])
+        edge[count[0] % 2, 0:end_size(l)] = pack(tile, FOLD_END[l])
 
     def send(k, l, v):
         r = nrow[l]
@@ -177,10 +172,10 @@
         else:
             size = row_size(l)
             for side, at in ((0, 1), (1, r)):
-                row_send[side, 0:size] = pack(jnp.where(lane < ncol[l], v[at], 0.0), FOLD_ROW[l])
-            rows = (row_send.at[0, pl.ds(0, size)], row_send.at[1, pl.ds(0, size)])
+                row_send[k % 2, side, 0:size] = pack(jnp.where(lane < ncol[l], v[at], 0.0), FOLD_ROW[l])
+            rows = (row_send.at[k % 2, 0, pl.ds(0, size)], row_send.at[k % 2, 1, pl.ds(0, size)])
         size = end_size(l)
-        ends_ref = edge.at[pl.ds(0, size)]
+        ends_ref = edge.at[k % 2, pl.ds(0, size)]
         copies = []
         for ref, to, slot in ((rows[0], 0, 1), (rows[1], 1, 0), (ends_ref, 2, 3), (ends_ref, 3, 2)):
             count_z = row_size(l) if to < 2 else size
@@ -188,6 +183,9 @@
                 src_ref=ref, dst_ref=held.at[k, slot, pl.ds(0, count_z)], send_sem=send_sem.at[k, slot],
                 recv_sem=recv_sem.at[k, slot], device_id=peers[to], device_id_type=MESH))
             copies[-1].start()
+        for copy in leaving:
+            copy.wait_send()
+        leaving[:] = copies
         return copies
 
     def partial(l, v, x):
@@ -217,7 +215,6 @@
         beside = unpack(both, jnp.where(odd, from_low, from_high), keep, depth, FOLD_END[l])
         return low, high, beside
 
-    count = [0]
 
     tail = jnp.zeros((depth - nz, LANES), F32)
 
@@ -258,7 +255,7 @@
             return acc
         put_ends(l, each_group(l, body, jnp.zeros((depth, LANES), F32)))
 
-    def relax(l, v, w, pending=None, start=False):
+    def relax(l, v, w, pending=None, start=False, last=False):
         k = count[0]
         count[0] += 1
         copies = send(k, l, v)
@@ -272,19 +269,22 @@
             for j in range(g):
                 row = parts[j][1] + d[:, j * LANES:(j + 1) * LANES]
                 w[x0 + j + 1] = row
-                acc = extract(acc, row, x0 + j, ncol[l])
+                if not last:
+                    acc = extract(acc, row, x0 + j, ncol[l])
             return acc
 
         acc = each_group(l, body, jnp.zeros((depth, LANES), F32))
         if start:
             coarse_coef()
         for copy in copies:
-            copy.wait()
+            copy.wait_recv()
         r, c = nrow[l], ncol[l]
         corr = block_dot(binv_ref[l, :, 0:3 * depth + 8], jnp.concatenate(halos(k, l), axis=1))
         low, high, beside = (corr[:, j * LANES:(j + 1) * LANES] for j in range(3))
         w[1] = w[1] + low + insert(beside, 0, c)
         w[r] = w[r] + high + insert(beside, r - 1, c)
+        if last:
+            return beside
         acc = acc + beside
         zero = jnp.zeros_like(acc)
         acc = acc + extract(zero, low, 0, c) + extract(zero, high, r - 1, c)
@@ -300,7 +300,7 @@
             v[i + 2] = v[i + 2] + insert(beside, i + 1, c)
             return acc
 
-        row_loop(nrow[l] - 2, 2 if nrow[l] > 6 else nrow[l], body)
+        row_loop(nrow[l] - 2, body)
 
     def residual(l, v, w, pending):
         k = count[0]
@@ -315,7 +315,7 @@
 
         each_group(l, body)
         for copy in copies:
-            copy.wait()
+            copy.wait_recv()
         r, c = nrow[l], ncol[l]
         low, high, beside = halos(k, l)
         w[1] = w[1] + low
@@ -327,7 +327,7 @@
             src[l + 1][i] = restrict(pair, l)
             return acc
 
-        row_loop(r // 2, 3, fold)
+        row_loop(r // 2, fold)
 
     def add_coarse(l, v, coarse):
         def body(x, acc):
@@ -338,7 +338,7 @@
                 acc = extract(acc, row, j, ncol[l])
             return acc
 
-        put_ends(l, row_loop(nrow[l + 1], 3, body, jnp.zeros((depth, LANES), F32)))
+        put_ends(l, row_loop(nrow[l + 1], body, jnp.zeros((depth, LANES), F32)))
 
     def cycle(l):
         a, b = va[l], vb[l]
@@ -350,23 +350,30 @@
         if l == LEVELS - 1:
             p = relax(l, a, b)
             p = relax(l, b, a, p)
-            p = relax(l, a, b, p)
+            p = relax(l, a, b, p, last=True)
             settle(l, b, p)
             return b
         p = relax(l, a, b, start=l == 0)
         residual(l, b, a, p)
         add_coarse(l, b, cycle(l + 1))
         p = relax(l, b, a)
-        p = relax(l, a, b, p)
+        p = relax(l, a, b, p, last=True)
+        if l == 0:
+            return b, p
         settle(l, b, p)
         return b
 
-    v = cycle(0)
+    v, rest = cycle(0)
     stores = []
     for x in range(rows0):
-        stage_s[x] = v[x + 1][0:nz]
+        row = v[x + 1]
+        if 0 < x < rows0 - 1:
+            row = row + insert(rest, x, ncol[0])
+        stage_s[x] = row[0:nz]
         stores.append(pltpu.make_async_copy(stage_s.at[x], out_ref.at[:, x, 0, :], io_sem.at[0, x]))
         stores[-1].start()
+    for copy in leaving:
+        copy.wait_send()
     for store in stores:
         store.wait()
 
@@ -391,13 +398,13 @@
         scratch_shapes=[
             pltpu.VMEM((rows, nz, LANES), F32),
             pltpu.VMEM((rows, nz, LANES), F32),
-            pltpu.VMEM((2, depth, LANES), F32),
+            pltpu.VMEM((2, 2, depth, LANES), F32),
             pltpu.VMEM((3, depth, LANES), F32),
             pltpu.VMEM((LEVELS, depth, LANES), F32),
             pltpu.VMEM((LEVELS, depth, 2 * LANES), BF),
             pltpu.SemaphoreType.DMA((2, rows)),
         ] + [tile(r + 2) for r in rl] * 2 + [tile(r) for r in rl] * 2 + [
-            pltpu.VMEM((depth, LANES), F32),
+            pltpu.VMEM((2, depth, LANES), F32),
             pltpu.VMEM((steps, 4, depth, LANES), F32),
             pltpu.SemaphoreType.DMA((steps, 4)),
             pltpu.SemaphoreType.DMA((steps, 4)),

time: 73 us -> 70.4 us (0.964)
  Pallas kernels: 70.6 us -> 68 us
    pallas_call x1, Pallas kernels: 70.6 us -> 68 us  [on_device(): pl.pallas_call(functools.partial(kernel, n_gx, n_gy, rows, depth), out_sh...]
where the time goes in v5:
time: 70.4 us; the launch traced here: 70.1 us
  Pallas kernels  68 us (97%)
  local copies, waits for them, and re-layouts  2.12 us (3%)
    pallas_call x1, Pallas kernels, on_device(): pl.pallas_call(functools.partial(kernel, n_gx, n_gy, rows, depth), out_sh...  68 us
    unnamed x1, local copies, waits for them, and re-layouts  2.12 us

profile of v5, /device:TPU:0, one launch (start us, length us, event | category | flops | bytes accessed | tf_op | source)
XLA Modules:
  0.0 70.1 jit_solution(10022580748672958240)
XLA Ops:
  0.0 68.0 %shard_map.55 = f32[70,24,1,128]{3,2,1,0:T(1,128)} custom-call(s32[1,1,4]{2,1,0:T(1,128)} %flip_ref.1, f32[70,24,1,128]{3,2,1,0:T(1,128)} %bitcast.6, f32[70,24,1,128]{3,2,1,0:T(1,128)} %bitcast.7, f32[1,71]{1,0:T(1,128)} %bitcast.9, f32[5,14,4,14]{3,2,1,0:T(4,128)} %bitcast.8), custom_call_target="tpu_custom_call" | custom-call | tf_op jit(solution)/shard_map/pallas_call | solution.py:393
  68.0 2.1 %copy.7 = f32[70,24,128]{2,1,0:T(8,128)} copy(f32[70,24,128]{2,1,0:T(8,128)} %bitcast.5) | data formatting | bytes 1720320

commit v6 on v5

--- a/solution.py
+++ b/solution.py
@@ -122,7 +122,7 @@
             buf[nrow[l] + 1] = jnp.zeros((depth, LANES), F32)
 
     group = [4, 4, 3, 3]
-    per_step = [8, 12, 6, 3]
+    per_step = [24, 12, 6, 3]
 
     def each_group(l, body, carry=0):
         g = group[l] if nrow[l] % group[l] == 0 else 1

time: 70.4 us -> 70.5 us (level)
  no operation moved by 1% of the time
where the time goes in v6:
time: 70.5 us; the launch traced here: 70.3 us
  Pallas kernels  68.1 us (97%)
  local copies, waits for them, and re-layouts  2.12 us (3%)
    pallas_call x1, Pallas kernels, on_device(): pl.pallas_call(functools.partial(kernel, n_gx, n_gy, rows, depth), out_sh...  68.1 us
    unnamed x1, local copies, waits for them, and re-layouts  2.12 us

profile of v6, /device:TPU:0, one launch (start us, length us, event | category | flops | bytes accessed | tf_op | source)
XLA Modules:
  0.0 70.3 jit_solution(12632002730321157809)
XLA Ops:
  0.0 68.1 %shard_map.55 = f32[70,24,1,128]{3,2,1,0:T(1,128)} custom-call(s32[1,1,4]{2,1,0:T(1,128)} %flip_ref.1, f32[70,24,1,128]{3,2,1,0:T(1,128)} %bitcast.6, f32[70,24,1,128]{3,2,1,0:T(1,128)} %bitcast.7, f32[1,71]{1,0:T(1,128)} %bitcast.9, f32[5,14,4,14]{3,2,1,0:T(4,128)} %bitcast.8), custom_call_target="tpu_custom_call" | custom-call | tf_op jit(solution)/shard_map/pallas_call | solution.py:393
  68.2 2.1 %copy.7 = f32[70,24,128]{2,1,0:T(8,128)} copy(f32[70,24,128]{2,1,0:T(8,128)} %bitcast.5) | data formatting | bytes 1720320
